TPU v7x, 32 devices: a whole 2x2x4 slice. The times are simulated.
32 devices in a mesh: expert: 16 (over z, y, x), pair: 2 (over core).
Axes of the slice: x: 2, y: 2, z: 4, core: 2. Of those that a mesh axis runs over, the one named last changes fastest.
Arguments:
- tokens: bfloat16 [4096, 2048], P(('expert', 'pair')), may hold values from -6 to 6
- out_grads: bfloat16 [4096, 2048], P(('expert', 'pair')), may hold values from -60 to 60
- routing: int32 [4096, 8], P(('expert', 'pair')), may hold values from 0 to 15, all different within a row; in each aligned block of 128 rows (0 to 127, 128 to 255, ...) at most 81 rows name the same one
- combine: float32 [4096, 8], P(('expert', 'pair')), may hold values from 0.05 to 0.3
- weights: bfloat16 [2, 16, 768, 2048], P('pair', 'expert'), may hold values from -6 to 6
- momentum: float32 [2, 16, 768, 2048], P('pair', 'expert'), may hold values from -40 to 40
Outputs:
- momentum_out: float32 [2, 16, 768, 2048], P('pair', 'expert')
- rollout_weights: bfloat16 [2, 16, 768, 2048], P(None, 'expert', 'pair')
Inputs may be any that keep to these rules, and one draw needn't show every extreme that they name: `routing`: each row names 8 different experts; within the 128 rows of one device no expert is named more than 81 times, and in some device's rows some expert is named exactly 81 times.
All inputs are finite; a program needn't handle non-finite values.
Results may differ from a plain program's by a relative error of at most 0.005.
Values may be sent and summed in bfloat16 or wider, within the bound.
A program may use at most 128 MiB of HBM per device.

v0:
```python
import math

import jax
import jax.numpy as jnp
from jax import lax
from jax.sharding import PartitionSpec as P

D = 2048
FF = 768
NS_ITERS = 2


COEF_A = 3.4445
COEF_B = -4.775
COEF_C = 2.0315
DECAY = 0.9
NORM_EPS = 1e-07


def contract_last(left_side, right_side):
    return lax.dot_general(
        left_side, right_side, (((1,), (1,)), ((), ())), preferred_element_type=jnp.float32
    )


def contract_first(left_side, right_side):
    return lax.dot_general(
        left_side, right_side, (((0,), (0,)), ((), ())), preferred_element_type=jnp.float32
    )


def forward_pre(x_rows, up_weight):
    return contract_last(x_rows, up_weight) * (1.0 / math.sqrt(D))


def up_gradient(x_rows, scaled_rows, pre_act, down_weight):
    squash = jax.nn.sigmoid(pre_act)
    hidden_grad = contract_last(scaled_rows, down_weight) * (1.0 / math.sqrt(FF))
    pre_grad = (hidden_grad * squash * (1.0 + pre_act * (1.0 - squash))).astype(jnp.bfloat16)
    return contract_first(pre_grad, x_rows) * (1.0 / math.sqrt(D))


def down_gradient(scaled_rows, pre_act):
    hidden = (pre_act * jax.nn.sigmoid(pre_act)).astype(jnp.bfloat16)
    return contract_first(hidden, scaled_rows) * (1.0 / math.sqrt(FF))


def newton_schulz(matrix):
    frobenius = jnp.sqrt(jnp.sum(matrix * matrix))
    orthogonal = (matrix / (frobenius + NORM_EPS)).astype(jnp.bfloat16)
    for iteration in range(NS_ITERS):
        gram_matrix = contract_last(orthogonal, orthogonal).astype(jnp.bfloat16)
        square = jnp.dot(gram_matrix, gram_matrix, preferred_element_type=jnp.float32)
        polynomial = (COEF_B * gram_matrix.astype(jnp.float32) + COEF_C * square).astype(
            jnp.bfloat16
        )
        orthogonal = (
            COEF_A * orthogonal.astype(jnp.float32)
            + jnp.dot(polynomial, orthogonal, preferred_element_type=jnp.float32)
        ).astype(jnp.bfloat16)
    return orthogonal


def on_device(tokens, out_grads, routing, combine, weights, momentum):
    tok_rows, model_width = tokens.shape
    top_count = routing.shape[1]
    n_expert = lax.axis_size("expert")
    capacity = tok_rows * top_count * 5 // (4 * n_expert) + 1
    slot_count = n_expert * capacity
    flat_expert = routing.reshape(-1)
    one_hot = (flat_expert[:, None] == jnp.arange(n_expert, dtype=jnp.int32)[None, :]).astype(
        jnp.int32
    )
    earlier = jnp.cumsum(one_hot, axis=0) - one_hot
    position = jnp.sum(earlier * one_hot, axis=1)
    target = flat_expert * capacity + position
    source = jnp.arange(flat_expert.shape[0], dtype=jnp.int32) // top_count
    slot_token = jnp.zeros((slot_count,), jnp.int32).at[target].set(source)
    slot_weight = jnp.zeros((slot_count,), jnp.float32).at[target].set(combine.reshape(-1))
    filled = jnp.zeros((slot_count,), jnp.bool_).at[target].set(True)
    x_send = jnp.where(filled[:, None], tokens[slot_token], 0).reshape(
        n_expert, capacity, model_width
    )
    scaled_send = jnp.where(
        filled[:, None], out_grads[slot_token].astype(jnp.float32) * slot_weight[:, None], 0.0
    )
    scaled_send = scaled_send.astype(jnp.bfloat16).reshape(n_expert, capacity, model_width)
    paired = lax.all_gather(weights, "pair", axis=0, tiled=True)
    up_weight = paired[0, 0]
    down_weight = paired[1, 0]
    x_recv, scaled_recv = (
        lax.all_to_all(x_send, "expert", split_axis=0, concat_axis=0, tiled=True),
        lax.all_to_all(scaled_send, "expert", split_axis=0, concat_axis=0, tiled=True),
    )
    x_rows = x_recv.reshape(slot_count, model_width)
    pre_act = forward_pre(x_rows, up_weight)
    scaled_rows = scaled_recv.reshape(slot_count, model_width)
    grad_up = up_gradient(x_rows, scaled_rows, pre_act, down_weight)
    grad_down = down_gradient(scaled_rows, pre_act)
    summed = lax.psum_scatter(
        jnp.stack([grad_up, grad_down])[:, None].astype(jnp.bfloat16),
        "pair",
        scatter_dimension=0,
        tiled=True,
    ).astype(jnp.float32)[0, 0]
    velocity = DECAY * momentum[0, 0] + summed
    orthogonal = newton_schulz(velocity)
    step_size = 0.5 * math.sqrt(D)
    updated = (
        weights[0, 0].astype(jnp.float32) - step_size * orthogonal.astype(jnp.float32)
    ).astype(jnp.bfloat16)
    rollout = lax.all_to_all(updated[None, None], "pair", split_axis=2, concat_axis=0, tiled=True)
    return (velocity[None, None], rollout)


def solution(mesh):
    return jax.shard_map(
        on_device,
        mesh=mesh,
        in_specs=(
            P(("expert", "pair"), None),
            P(("expert", "pair"), None),
            P(("expert", "pair"), None),
            P(("expert", "pair"), None),
            P("pair", "expert", None, None),
            P("pair", "expert", None, None),
        ),
        out_specs=(P("pair", "expert", None, None), P(None, "expert", "pair", None)),
        check_vma=False,
    )
```

profile of v0, /device:TPU:0, one launch (start us, length us, event | category | flops | bytes accessed | tf_op | source)
XLA Modules:
  0.0 494.2 jit_solution(11353786528073871296)
XLA Ops:
  18.5 6.6 %gather_fusion = bf16[1296,2048]{1,0:T(8,128)(2,1)} fusion(bf16[128,2048]{1,0:T(8,128)(2,1)S(1)} %copy-done, s32[2048]{0:T(1024)S(1)} %pad_clamp_fusion), kind=kCustom, calls=%fused_computation | custom fusion | bytes 10622016 | tf_op jit(solution)/shard_map/gather | solution.py:85
  25.1 9.9 %reshape.133 = f32[16,81,2048]{2,1,0:T(8,128)} reshape(bf16[1296,2048]{1,0:T(8,128)(2,1)} %gather_fusion) | data formatting | bytes 15925248 | tf_op jit(solution)/shard_map/convert_element_type | solution.py:85
  44.0 7.9 %select_convert_fusion = bf16[16,81,2048]{2,1,0:T(8,128)(2,1)} fusion(f32[16,81,2048]{2,1,0:T(8,128)} %reshape.133, f32[16,81]{1,0:T(8,128)S(1)} %mul.110, pred[16,81]{1,0:T(8,128)(4,1)S(1)} %broadcast_in_dim.51), kind=kLoop, calls=%fused_computation.5 | loop fusion | flops 7962624 | bytes 15931728 | tf_op jit(solution)/shard_map/convert_element_type | solution.py:87
  51.9 9.0 %all-to-all-start = ((bf16[16,81,2048]{2,1,0:T(8,128)(2,1)}), bf16[16,81,2048]{2,1,0:T(8,128)(2,1)}, u32[]{:S(2)}, u32[]{:S(2)}) async-start(bf16[16,81,2048]{2,1,0:T(8,128)(2,1)} %select_convert_fusion), calls=%async_computation | async-start | bytes 11534336 | tf_op jit(solution)/shard_map/all_to_all | solution.py:93
  60.9 6.7 %gather_fusion.1 = bf16[1296,2048]{1,0:T(8,128)(2,1)} fusion(bf16[128,2048]{1,0:T(8,128)(2,1)S(1)} %copy-done.2, s32[2048]{0:T(1024)S(1)} %pad_clamp_fusion), kind=kCustom, calls=%fused_computation.1 | custom fusion | bytes 10622016 | tf_op jit(solution)/shard_map/gather | solution.py:81
  72.6 5.6 %broadcast_select_fusion = bf16[16,81,2048]{2,1,0:T(8,128)(2,1)} fusion(bf16[16,81,2048]{2,1,0:T(8,128)(2,1)} %gather.10, pred[16,81]{1,0:T(8,128)(4,1)S(1)} %broadcast_in_dim.51), kind=kLoop, calls=%fused_computation.16 | loop fusion | flops 2654208 | bytes 10618128 | tf_op jit(solution)/shard_map/jit(_where)/select_n | solution.py:81
  78.2 91.2 %all-to-all-done = bf16[16,81,2048]{2,1,0:T(8,128)(2,1)} async-done(((bf16[16,81,2048]{2,1,0:T(8,128)(2,1)}), bf16[16,81,2048]{2,1,0:T(8,128)(2,1)}, u32[]{:S(2)}, u32[]{:S(2)}) %all-to-all-start) | async-done | bytes 5308448 | tf_op jit(solution)/shard_map/all_to_all | solution.py:93
  169.3 27.2 %all-to-all-start.1 = ((bf16[16,81,2048]{2,1,0:T(8,128)(2,1)}), bf16[16,81,2048]{2,1,0:T(8,128)(2,1)}, u32[]{:S(2)}, u32[]{:S(2)}) async-start(bf16[16,81,2048]{2,1,0:T(8,128)(2,1)} %broadcast_select_fusion), calls=%async_computation.1 | async-start | bytes 11534336 | tf_op jit(solution)/shard_map/all_to_all | solution.py:92
  202.4 99.9 %all-to-all-done.1 = bf16[16,81,2048]{2,1,0:T(8,128)(2,1)} async-done(((bf16[16,81,2048]{2,1,0:T(8,128)(2,1)}), bf16[16,81,2048]{2,1,0:T(8,128)(2,1)}, u32[]{:S(2)}, u32[]{:S(2)}) %all-to-all-start.1) | async-done | bytes 5308448 | tf_op jit(solution)/shard_map/all_to_all | solution.py:92
  307.4 7.4 %convolution_multiply_fusion = f32[1296,768]{1,0:T(8,128)S(1)} fusion(bf16[1296,2048]{1,0:T(8,128)(2,1)} %reshape.132, bf16[2,1,768,2048]{3,2,1,0:T(8,128)(2,1)} %all-gather.2.cloned.1.call-done), kind=kOutput, calls=%fused_computation.17 | convolution fusion | flops 4077858816 | bytes 12435456 | tf_op jit(solution)/shard_map/dot_general | solution.py:21
  316.8 7.0 %fusion.9 = bf16[1,1,768,2048]{3,2,1,0:T(8,128)(2,1)} fusion(bf16[1296,2048]{1,0:T(8,128)(2,1)S(1)} %copy-done.3, f32[1296,768]{1,0:T(8,128)S(1)} %convolution_multiply_fusion), kind=kOutput, calls=%fused_computation.31 | convolution fusion | flops 4084985856 | bytes 12435456 | tf_op jit(solution)/shard_map/dot_general | solution.py:27
  323.7 25.6 %fusion.8 = bf16[1,1,768,2048]{3,2,1,0:T(8,128)(2,1)} fusion(bf16[1296,2048]{1,0:T(8,128)(2,1)} %reshape.132, f32[1296,768]{1,0:T(8,128)} %copy-done.5, bf16[1296,2048]{1,0:T(8,128)(2,1)} %reshape.131, bf16[2,1,768,2048]{3,2,1,0:T(8,128)(2,1)} %all-gather.2.cloned.1.call-done), kind=kOutput, calls=%fused_computation.30 | convolution fusion | flops 8166825984 | bytes 20889600 | tf_op jit(solution)/shard_map/dot_general | solution.py:27
  349.3 6.1 %pad_maximum_fusion = bf16[2,1,768,2048]{3,2,1,0:T(8,128)(2,1)} fusion(bf16[1,1,768,2048]{3,2,1,0:T(8,128)(2,1)} %fusion.9, bf16[1,1,768,2048]{3,2,1,0:T(8,128)(2,1)} %fusion.8), kind=kLoop, calls=%fused_computation.6 | loop fusion | flops 3145728 | bytes 12582912 | tf_op jit(solution)/shard_map/stack | solution.py:101
  355.5 35.1 %reduce-scatter.2.cloned.1.call-done = bf16[1,1,768,2048]{3,2,1,0:T(8,128)(2,1)} async-done(((bf16[2,1,768,2048]{3,2,1,0:T(8,128)(2,1)}), bf16[1,1,768,2048]{3,2,1,0:T(8,128)(2,1)}) %reduce-scatter.2.cloned.1.call-update) | async-done | bytes 3145744 | tf_op jit(solution)/shard_map/reduce_scatter | solution.py:100
  390.6 8.8 %multiply_reduce_fusion = (f32[]{:T(128)}, f32[1,1,768,2048]{3,2,1,0:T(8,128)}) fusion(bf16[1,1,768,2048]{3,2,1,0:T(8,128)(2,1)} %reduce-scatter.2.cloned.1.call-done, f32[1,1,768,2048]{3,2,1,0:T(8,128)} %param.11), kind=kLoop, calls=%fused_computation.12 | loop fusion | flops 7864319 | bytes 15728644 | tf_op jit(solution)/shard_map/reduce_sum | solution.py:49
  400.1 7.3 %fusion.11 = bf16[768,768]{1,0:T(8,128)(2,1)S(1)} fusion(f32[1,1,768,2048]{3,2,1,0:T(8,128)} %get-tuple-element.11, f32[]{:T(128)S(6)} %add.64), kind=kOutput, calls=%fused_computation.35 | convolution fusion | flops 2419654656 | bytes 7471108 | tf_op jit(solution)/shard_map/dot_general | solution.py:21
  407.3 9.5 %add_convert_fusion.1 = bf16[768,2048]{1,0:T(8,128)(2,1)} fusion(bf16[768,768]{1,0:T(8,128)(2,1)S(1)} %fusion.11, f32[1,1,768,2048]{3,2,1,0:T(8,128)} %get-tuple-element.11, f32[]{:T(128)S(6)} %add.64), kind=kOutput, calls=%fused_computation.10 | convolution fusion | flops 3337420800 | bytes 10616836 | tf_op jit(solution)/shard_map/dot_general | solution.py:59
  416.8 5.5 %convolution_convert_fusion = bf16[768,768]{1,0:T(8,128)(2,1)S(1)} fusion(bf16[768,2048]{1,0:T(8,128)(2,1)} %add_convert_fusion.1), kind=kOutput, calls=%fused_computation.36 | convolution fusion | flops 2416508928 | bytes 4325376 | tf_op jit(solution)/shard_map/dot_general | solution.py:21
  422.3 9.1 %fusion.4 = bf16[1,1,768,2048]{3,2,1,0:T(8,128)(2,1)} fusion(bf16[1,1,768,2048]{3,2,1,0:T(8,128)(2,1)} %param.10, bf16[768,2048]{1,0:T(8,128)(2,1)} %add_convert_fusion.1, bf16[768,768]{1,0:T(8,128)(2,1)S(1)} %convolution_convert_fusion), kind=kOutput, calls=%fused_computation.24 | convolution fusion | flops 3338993664 | bytes 10616832 | tf_op jit(solution)/shard_map/dot_general | solution.py:59
  431.5 7.0 %copy.38 = bf16[1,1,768,2048]{3,1,0,2:T(2,128)(2,1)} copy(bf16[1,1,768,2048]{3,2,1,0:T(8,128)(2,1)} %fusion.4) | data formatting | bytes 6291456 | tf_op jit(solution)/shard_map/broadcast_in_dim | solution.py:112
  439.0 20.5 %reduce.1 = bf16[768,2048]{1,0:T(8,128)(2,1)} reduce(bf16[768,1,1,2048]{3,2,1,0:T(2,128)(2,1)} %bitcast.62, bf16[]{:T(256)} %broadcast.137), dimensions={1,2}, to_apply=%bitcast.61.reduce_sub_computation | reduce | bytes 6291458
  464.3 10.3 %all_to_all.22 = bf16[2,2,393216]{2,1,0:T(2,128)(2,1)} all-to-all(bf16[2,2,393216]{2,1,0:T(2,128)(2,1)} %reshape.183), channel_id=1, replica_groups=mesh['expert'=16,'pair'=2] {'pair'}, dimensions={0} | all-to-all | bytes 6291456 | tf_op jit(solution)/shard_map/all_to_all | solution.py:112
  474.6 5.8 %reshape.184 = bf16[768,1,1,2048]{3,2,1,0:T(2,128)(2,1)} reshape(bf16[2,2,393216]{2,1,0:T(2,128)(2,1)} %all_to_all.22) | data formatting | bytes 6291456
  480.4 6.5 %copy.34 = bf16[1,1,768,2048]{3,2,0,1:T(8,128)(2,1)} copy(bf16[1,1,768,2048]{3,1,0,2:T(2,128)(2,1)} %bitcast.63) | data formatting | bytes 6291456
  (49 shorter events, 43.5 us)
Async XLA Ops:
  7.2 11.3 %copy-start = (bf16[128,2048]{1,0:T(8,128)(2,1)S(1)}, bf16[128,2048]{1,0:T(8,128)(2,1)}, u32[]{:S(2)}) copy-start(bf16[128,2048]{1,0:T(8,128)(2,1)} %param.7) | copy-start | bytes 1572868
  25.1 14.3 %copy-start.4 = (f32[128,8]{0,1:T(8,128)S(1)}, f32[128,8]{0,1:T(8,128)}, u32[]{:S(2)}) copy-start(f32[128,8]{0,1:T(8,128)} %param.9) | copy-start | bytes 12292
  51.9 9.0 %copy-start.2 = (bf16[128,2048]{1,0:T(8,128)(2,1)S(1)}, bf16[128,2048]{1,0:T(8,128)(2,1)}, u32[]{:S(2)}) copy-start(bf16[128,2048]{1,0:T(8,128)(2,1)} %param.6) | copy-start | bytes 1572868
  51.9 117.4 %all-to-all-start = ((bf16[16,81,2048]{2,1,0:T(8,128)(2,1)}), bf16[16,81,2048]{2,1,0:T(8,128)(2,1)}, u32[]{:S(2)}, u32[]{:S(2)}) async-start(bf16[16,81,2048]{2,1,0:T(8,128)(2,1)} %select_convert_fusion), calls=%async_computation | async-start | bytes 11534336 | tf_op jit(solution)/shard_map/all_to_all | solution.py:93
  169.3 133.0 %all-to-all-start.1 = ((bf16[16,81,2048]{2,1,0:T(8,128)(2,1)}), bf16[16,81,2048]{2,1,0:T(8,128)(2,1)}, u32[]{:S(2)}, u32[]{:S(2)}) async-start(bf16[16,81,2048]{2,1,0:T(8,128)(2,1)} %broadcast_select_fusion), calls=%async_computation.1 | async-start | bytes 11534336 | tf_op jit(solution)/shard_map/all_to_all | solution.py:92
  196.6 110.8 %all-gather.2.cloned.1.call-start = ((), (), s32[]{:S(2)}) async-start(), calls=%async_computation.4 | async-start | bytes 9437184 | tf_op jit(solution)/shard_map/all_gather | solution.py:88
  197.3 193.3 %reduce-scatter.2.cloned.1.call-start = ((), (), s32[]{:S(2)}) async-start(), calls=%async_computation.5 | async-start | bytes 9437184 | tf_op jit(solution)/shard_map/reduce_scatter | solution.py:100
  307.4 9.4 %copy-start.3 = (bf16[1296,2048]{1,0:T(8,128)(2,1)S(1)}, bf16[1296,2048]{1,0:T(8,128)(2,1)}, u32[]{:S(2)}) copy-start(bf16[1296,2048]{1,0:T(8,128)(2,1)} %reshape.131) | copy-start | bytes 15925252
  314.8 2.0 copy-start.5
  480.4 6.5 %copy-start.1 = (bf16[128,2048]{1,0:T(8,128)(2,1)S(1)}, bf16[128,2048]{1,0:T(8,128)(2,1)}, u32[]{:S(2)}) copy-start(bf16[128,2048]{1,0:T(8,128)(2,1)} %param.7) | copy-start | bytes 1572868
Sparse Core Ops, SparseCore 0:
  199.0 17.9 all-gather.1
  355.6 34.9 reduce-scatter.1
where the time goes:
time: 502 us; the launch traced here: 494 us
  waiting for transfers between devices  227 us (45%)
  local copies, waits for them, and re-layouts  79.7 us (16%)
  matrix products  71.3 us (14%)
  other arithmetic  54.2 us (11%)
  starting transfers between devices  36.3 us (7%)
  between operations  15.4 us (3%)
  blocking collectives  10.3 us (2%)
    all_to_all x1, waiting for transfers between devices, on_device(): lax.all_to_all(x_send, 'expert', split_axis=0, concat_axis=0, tiled=True)  99.9 us
    all_to_all x1, waiting for transfers between devices, on_device(): lax.all_to_all(scaled_send, 'expert', split_axis=0, concat_axis=0, tiled=...  91.2 us
    reduce_scatter x1, waiting for transfers between devices, on_device(): lax.psum_scatter(jnp.stack([grad_up, grad_down])[:, None].astype(jnp.bflo...  35.1 us
    dot_general x2, matrix products, contract_first(): lax.dot_general(left_side, right_side, (((0,), (0,)), ((), ())), preferre...  32.5 us
    all_to_all x1, starting transfers between devices, on_device(): lax.all_to_all(x_send, 'expert', split_axis=0, concat_axis=0, tiled=True)  27.2 us
    unnamed x18, local copies, waits for them, and re-layouts  20.5 us
    unnamed x1, other arithmetic  20.5 us
    dot_general x3, matrix products, contract_last(): lax.dot_general(left_side, right_side, (((1,), (1,)), ((), ())), preferre...  20.1 us
  transfers between devices with their start and end apart: 4, of which 3 were waited for; matrix products, arithmetic and copies ran while one was open for 6% of the time, Pallas kernels for 0%

commit v1 on v0

--- a/solution.py
+++ b/solution.py
@@ -15,6 +15,7 @@
 COEF_C = 2.0315
 DECAY = 0.9
 NORM_EPS = 1e-07
+GATHER_LIMIT = 24 << 20
 
 
 def contract_last(left_side, right_side):
@@ -61,7 +62,7 @@
     return orthogonal
 
 
-def on_device(tokens, out_grads, routing, combine, weights, momentum):
+def sparse_rows(tokens, out_grads, routing, combine):
     tok_rows, model_width = tokens.shape
     top_count = routing.shape[1]
     n_expert = lax.axis_size("expert")
@@ -85,16 +86,32 @@
         filled[:, None], out_grads[slot_token].astype(jnp.float32) * slot_weight[:, None], 0.0
     )
     scaled_send = scaled_send.astype(jnp.bfloat16).reshape(n_expert, capacity, model_width)
-    paired = lax.all_gather(weights, "pair", axis=0, tiled=True)
-    up_weight = paired[0, 0]
-    down_weight = paired[1, 0]
     x_recv, scaled_recv = (
         lax.all_to_all(x_send, "expert", split_axis=0, concat_axis=0, tiled=True),
         lax.all_to_all(scaled_send, "expert", split_axis=0, concat_axis=0, tiled=True),
     )
-    x_rows = x_recv.reshape(slot_count, model_width)
+    return x_recv.reshape(slot_count, model_width), scaled_recv.reshape(slot_count, model_width)
+
+
+def dense_rows(tokens, out_grads, routing, combine):
+    n_expert = lax.axis_size("expert")
+    names = jnp.arange(n_expert, dtype=jnp.int32)[:, None, None]
+    row_weight = jnp.sum(jnp.where(routing[None] == names, combine[None], 0.0), axis=2)
+    row_weight = lax.all_to_all(row_weight, "expert", split_axis=0, concat_axis=0, tiled=True)
+    x_rows = lax.all_gather(tokens, "expert", axis=0, tiled=True)
+    grad_rows = lax.all_gather(out_grads, "expert", axis=0, tiled=True)
+    scaled_rows = (grad_rows.astype(jnp.float32) * row_weight.reshape(-1, 1)).astype(jnp.bfloat16)
+    return x_rows, scaled_rows
+
+
+def on_device(tokens, out_grads, routing, combine, weights, momentum):
+    paired = lax.all_gather(weights, "pair", axis=0, tiled=True)
+    up_weight = paired[0, 0]
+    down_weight = paired[1, 0]
+    gathered_bytes = 2 * tokens.size * tokens.dtype.itemsize * lax.axis_size("expert")
+    collect = dense_rows if gathered_bytes <= GATHER_LIMIT else sparse_rows
+    x_rows, scaled_rows = collect(tokens, out_grads, routing, combine)
     pre_act = forward_pre(x_rows, up_weight)
-    scaled_rows = scaled_recv.reshape(slot_count, model_width)
     grad_up = up_gradient(x_rows, scaled_rows, pre_act, down_weight)
     grad_down = down_gradient(scaled_rows, pre_act)
     summed = lax.psum_scatter(

time: 502 us -> 428 us (0.85)
  local copies, waits for them, and re-layouts: 79.7 us -> 23.2 us
  starting transfers between devices: 36.3 us -> 8.47 us
  matrix products: 71.3 us -> 93.4 us
  other arithmetic: 54.2 us -> 34 us
  waiting for transfers between devices: 227 us -> 243 us
    all_gather x0 -> x2, waiting for transfers between devices: none -> 218 us  [the longest x1 117 us: dense_rows(): x_rows = lax.all_gather(tokens, 'expert', axis=0, tiled=True)]
    all_to_all x2 -> x1, waiting for transfers between devices: 191 us -> 0.01 us  [dense_rows(): lax.all_to_all(row_weight, 'expert', split_axis=0, concat_axis=0, tiled=T...]
    all_to_all x2 -> x1, starting transfers between devices: 36.2 us -> 8.31 us  [dense_rows(): lax.all_to_all(row_weight, 'expert', split_axis=0, concat_axis=0, tiled=T...]
    reduce_scatter x1, waiting for transfers between devices: 35.1 us -> 12.8 us  [on_device(): lax.psum_scatter(jnp.stack([grad_up, grad_down])[:, None].astype(jnp.bflo...]
    gather x3 -> x0, local copies, waits for them, and re-layouts: 18.4 us -> none  [the longest x2 11.7 us: on_device(): tokens[slot_token]]
    dot_general x2, matrix products: 32.5 us -> 48.1 us  [contract_first(): lax.dot_general(left_side, right_side, (((0,), (0,)), ((), ())), preferre...]
    scatter x3 -> x0, local copies, waits for them, and re-layouts: 13 us -> none  [the longest x1 4.34 us: on_device(): filled = jnp.zeros((slot_count,), jnp.bool_).at[target].set(True)]
    reshape x3 -> x0, local copies, waits for them, and re-layouts: 10.2 us -> none  [the longest x1 5.06 us: on_device(): x_rows = x_recv.reshape(slot_count, model_width)]
  transfers between devices with their start and end apart: 4 -> 5, of which waited for: 3 -> 4; matrix products, arithmetic and copies ran while one was open for 6% -> 3% of each run, Pallas kernels for 0% -> 0%
where the time goes in v1:
time: 428 us; the launch traced here: 425 us
  waiting for transfers between devices  243 us (57%)
  matrix products  93.4 us (22%)
  other arithmetic  34 us (8%)
  local copies, waits for them, and re-layouts  23.2 us (5%)
  between operations  15 us (4%)
  starting transfers between devices  8.47 us (2%)
  blocking collectives  7.49 us (2%)
    all_gather x1, waiting for transfers between devices, dense_rows(): x_rows = lax.all_gather(tokens, 'expert', axis=0, tiled=True)  117 us
    all_gather x1, waiting for transfers between devices, dense_rows(): grad_rows = lax.all_gather(out_grads, 'expert', axis=0, tiled=True)  102 us
    dot_general x2, matrix products, contract_first(): lax.dot_general(left_side, right_side, (((0,), (0,)), ((), ())), preferre...  48.1 us
    dot_general x3, matrix products, contract_last(): lax.dot_general(left_side, right_side, (((1,), (1,)), ((), ())), preferre...  26.1 us
    unnamed x1, other arithmetic  20.6 us
    dot_general x2, matrix products, newton_schulz(): jnp.dot(polynomial, orthogonal, preferred_element_type=jnp.float32)  19.2 us
    unnamed x6, local copies, waits for them, and re-layouts  16.4 us
    reduce_scatter x1, waiting for transfers between devices, on_device(): lax.psum_scatter(jnp.stack([grad_up, grad_down])[:, None].astype(jnp.bflo...  12.8 us
  transfers between devices with their start and end apart: 5, of which 4 were waited for; matrix products, arithmetic and copies ran while one was open for 3% of the time, Pallas kernels for 0%

profile of v1, /device:TPU:0, one launch (start us, length us, event | category | flops | bytes accessed | tf_op | source)
XLA Modules:
  0.0 424.8 jit_solution(11089721645941106989)
XLA Ops:
  7.2 0.7 all-gather.6.cloned.1.call-update
  7.9 0.7 all-gather.8.cloned.1.call-update
  8.7 0.7 all-gather.4.cloned.1.call-update
  9.4 1.3 select_reduce_fusion
  10.7 8.3 %all-to-all-start = ((f32[16,1,128]{2,1,0:T(1,128)}), f32[16,1,128]{2,1,0:T(1,128)S(1)}, u32[]{:S(2)}, u32[]{:S(2)}) async-start(f32[16,1,128]{2,1,0:T(1,128)} %bitcast.1), calls=%async_computation | async-start | bytes 16384 | tf_op jit(solution)/shard_map/all_to_all | solution.py:100
  19.1 10.0 %all-gather.6.cloned.1.call-done = bf16[2,1,768,2048]{3,2,1,0:T(8,128)(2,1)} async-done(((bf16[1,1,768,2048]{3,2,1,0:T(8,128)(2,1)}), bf16[2,1,768,2048]{3,2,1,0:T(8,128)(2,1)}) %all-gather.6.cloned.1.call-update) | async-done | bytes 6291472 | tf_op jit(solution)/shard_map/all_gather | solution.py:108
  29.0 116.8 %all-gather.8.cloned.1.call-done = bf16[2048,2048]{1,0:T(8,128)(2,1)} async-done(((bf16[128,2048]{1,0:T(8,128)(2,1)}), bf16[2048,2048]{1,0:T(8,128)(2,1)}) %all-gather.8.cloned.1.call-update) | async-done | bytes 8388624 | tf_op jit(solution)/shard_map/all_gather | solution.py:101
  145.8 12.2 %fusion.3 = f32[2048,768]{1,0:T(8,128)} fusion(bf16[2048,2048]{1,0:T(8,128)(2,1)} %all-gather.8.cloned.1.call-done, bf16[2,1,768,2048]{3,2,1,0:T(8,128)(2,1)} %all-gather.6.cloned.1.call-done), kind=kOutput, calls=%fused_computation.17 | convolution fusion | flops 6442450944 | bytes 17825792 | tf_op jit(solution)/shard_map/dot_general | solution.py:22
  158.1 101.6 %all-gather.4.cloned.1.call-done = bf16[2048,2048]{1,0:T(8,128)(2,1)} async-done(((bf16[128,2048]{1,0:T(8,128)(2,1)}), bf16[2048,2048]{1,0:T(8,128)(2,1)}) %all-gather.4.cloned.1.call-update) | async-done | bytes 8388624 | tf_op jit(solution)/shard_map/all_gather | solution.py:102
  259.7 35.2 %fusion.12 = bf16[1,1,768,2048]{3,2,1,0:T(8,128)(2,1)S(1)} fusion(bf16[2048,2048]{1,0:T(8,128)(2,1)} %all-gather.8.cloned.1.call-done, f32[2048,768]{1,0:T(8,128)} %fusion.3, bf16[2048,2048]{1,0:T(8,128)(2,1)} %all-gather.4.cloned.1.call-done, f32[2048]{0:T(1024)S(1)} %bitcast.48, bf16[2,1,768,2048]{3,2,1,0:T(8,128)(2,1)} %all-gather.6.cloned.1.call-done), kind=kOutput, calls=%fused_computation.27 | convolution fusion | flops 12917932032 | bytes 29368320 | tf_op jit(solution)/shard_map/dot_general | solution.py:28
  294.9 12.8 %fusion.13 = bf16[1,1,768,2048]{3,2,1,0:T(8,128)(2,1)S(1)} fusion(bf16[2048,2048]{1,0:T(8,128)(2,1)} %all-gather.4.cloned.1.call-done, f32[2048]{0:T(1024)S(1)} %bitcast.49, f32[2048,768]{1,0:T(8,128)} %fusion.3), kind=kOutput, calls=%fused_computation.28 | convolution fusion | flops 6467616768 | bytes 17833984 | tf_op jit(solution)/shard_map/dot_general | solution.py:28
  307.8 3.2 pad_maximum_fusion
  311.0 12.8 %reduce-scatter.2.cloned.1.call-done = bf16[1,1,768,2048]{3,2,1,0:T(8,128)(2,1)} async-done(((bf16[2,1,768,2048]{3,2,1,0:T(8,128)(2,1)}), bf16[1,1,768,2048]{3,2,1,0:T(8,128)(2,1)}) %reduce-scatter.2.cloned.1.call-update) | async-done | bytes 3145744 | tf_op jit(solution)/shard_map/reduce_scatter | solution.py:117
  323.9 8.8 %multiply_reduce_fusion = (f32[]{:T(128)}, f32[1,1,768,2048]{3,2,1,0:T(8,128)}) fusion(bf16[1,1,768,2048]{3,2,1,0:T(8,128)(2,1)} %reduce-scatter.2.cloned.1.call-done, f32[1,1,768,2048]{3,2,1,0:T(8,128)} %param.11), kind=kLoop, calls=%fused_computation.7 | loop fusion | flops 7864319 | bytes 15728644 | tf_op jit(solution)/shard_map/reduce_sum | solution.py:50
  333.4 7.2 %fusion.14 = bf16[768,768]{1,0:T(8,128)(2,1)S(1)} fusion(f32[1,1,768,2048]{3,2,1,0:T(8,128)} %get-tuple-element.11, f32[]{:T(128)S(6)} %add.34), kind=kOutput, calls=%fused_computation.31 | convolution fusion | flops 2419654656 | bytes 7471108 | tf_op jit(solution)/shard_map/dot_general | solution.py:22
  340.6 9.7 %add_convert_fusion.1 = bf16[768,2048]{1,0:T(8,128)(2,1)} fusion(bf16[768,768]{1,0:T(8,128)(2,1)S(1)} %fusion.14, f32[1,1,768,2048]{3,2,1,0:T(8,128)} %get-tuple-element.11, f32[]{:T(128)S(6)} %add.34), kind=kOutput, calls=%fused_computation.5 | convolution fusion | flops 3337420800 | bytes 10616836 | tf_op jit(solution)/shard_map/dot_general | solution.py:60
  350.4 6.6 %convolution_convert_fusion = bf16[768,768]{1,0:T(8,128)(2,1)} fusion(bf16[768,2048]{1,0:T(8,128)(2,1)} %add_convert_fusion.1), kind=kOutput, calls=%fused_computation.32 | convolution fusion | flops 2416508928 | bytes 4325376 | tf_op jit(solution)/shard_map/dot_general | solution.py:22
  357.0 9.5 %fusion.2 = bf16[1,1,768,2048]{3,2,1,0:T(8,128)(2,1)} fusion(bf16[1,1,768,2048]{3,2,1,0:T(8,128)(2,1)S(1)} %copy-done, bf16[768,2048]{1,0:T(8,128)(2,1)} %add_convert_fusion.1, bf16[768,768]{1,0:T(8,128)(2,1)} %convolution_convert_fusion), kind=kOutput, calls=%fused_computation.15 | convolution fusion | flops 3338993664 | bytes 10616832 | tf_op jit(solution)/shard_map/dot_general | solution.py:60
  366.5 6.8 %copy.24 = bf16[1,1,768,2048]{3,1,0,2:T(2,128)(2,1)} copy(bf16[1,1,768,2048]{3,2,1,0:T(8,128)(2,1)} %fusion.2) | data formatting | bytes 6291456 | tf_op jit(solution)/shard_map/broadcast_in_dim | solution.py:129
  373.9 20.6 %reduce.1 = bf16[768,2048]{1,0:T(8,128)(2,1)} reduce(bf16[768,1,1,2048]{3,2,1,0:T(2,128)(2,1)} %bitcast.45, bf16[]{:T(256)} %broadcast.55), dimensions={1,2}, to_apply=%bitcast.44.reduce_sub_computation | reduce | bytes 6291458
  394.5 3.7 reshape.60
  398.2 7.5 %all_to_all.21 = bf16[2,2,393216]{2,1,0:T(2,128)(2,1)} all-to-all(bf16[2,2,393216]{2,1,0:T(2,128)(2,1)S(1)} %reshape.60), channel_id=1, replica_groups=mesh['expert'=16,'pair'=2] {'pair'}, dimensions={0} | all-to-all | bytes 6291456 | tf_op jit(solution)/shard_map/all_to_all | solution.py:129
  405.7 5.7 %reshape.61 = bf16[768,1,1,2048]{3,2,1,0:T(2,128)(2,1)} reshape(bf16[2,2,393216]{2,1,0:T(2,128)(2,1)} %all_to_all.21) | data formatting | bytes 6291456
  411.4 6.4 %copy.22 = bf16[1,1,768,2048]{3,2,0,1:T(8,128)(2,1)} copy(bf16[1,1,768,2048]{3,1,0,2:T(2,128)(2,1)} %bitcast.46) | data formatting | bytes 6291456
  (9 shorter events, 0.8 us)
Async XLA Ops:
  7.2 21.9 %all-gather.6.cloned.1.call-start = ((), (), s32[]{:S(2)}) async-start(), calls=%async_computation.4 | async-start | bytes 9437184 | tf_op jit(solution)/shard_map/all_gather | solution.py:108
  7.9 137.9 %all-gather.8.cloned.1.call-start = ((), (), s32[]{:S(2)}) async-start(), calls=%async_computation.5 | async-start | bytes 8912896 | tf_op jit(solution)/shard_map/all_gather | solution.py:101
  8.6 251.0 %all-gather.4.cloned.1.call-start = ((), (), s32[]{:S(2)}) async-start(), calls=%async_computation.3 | async-start | bytes 8912896 | tf_op jit(solution)/shard_map/all_gather | solution.py:102
  10.7 147.4 %all-to-all-start = ((f32[16,1,128]{2,1,0:T(1,128)}), f32[16,1,128]{2,1,0:T(1,128)S(1)}, u32[]{:S(2)}, u32[]{:S(2)}) async-start(f32[16,1,128]{2,1,0:T(1,128)} %bitcast.1), calls=%async_computation | async-start | bytes 16384 | tf_op jit(solution)/shard_map/all_to_all | solution.py:100
  19.0 304.8 %reduce-scatter.2.cloned.1.call-start = ((), (), s32[]{:S(2)}) async-start(), calls=%async_computation.6 | async-start | bytes 9437184 | tf_op jit(solution)/shard_map/reduce_scatter | solution.py:117
  350.4 6.7 %copy-start = (bf16[1,1,768,2048]{3,2,1,0:T(8,128)(2,1)S(1)}, bf16[1,1,768,2048]{3,2,1,0:T(8,128)(2,1)}, u32[]{:S(2)}) copy-start(bf16[1,1,768,2048]{3,2,1,0:T(8,128)(2,1)} %param.10) | copy-start | bytes 9437188
Sparse Core Ops, SparseCore 0:
  9.5 19.4 all-gather.5
  31.8 113.9 all-gather.7
  148.6 111.0 all-gather.3
  311.1 12.6 reduce-scatter.1

commit v2 on v0

--- a/solution.py
+++ b/solution.py
@@ -1,8 +1,11 @@
+import functools
 import math
 
 import jax
 import jax.numpy as jnp
 from jax import lax
+from jax.experimental import pallas as pl
+from jax.experimental.pallas import tpu as pltpu
 from jax.sharding import PartitionSpec as P
 
 D = 2048
@@ -15,6 +18,8 @@
 COEF_C = 2.0315
 DECAY = 0.9
 NORM_EPS = 1e-07
+GATHER_LIMIT = 24 << 20
+VMEM_BYTES = 60 << 20
 
 
 def contract_last(left_side, right_side):
@@ -61,7 +66,7 @@
     return orthogonal
 
 
-def on_device(tokens, out_grads, routing, combine, weights, momentum):
+def exchanged(tokens, out_grads, routing, combine, weights, momentum):
     tok_rows, model_width = tokens.shape
     top_count = routing.shape[1]
     n_expert = lax.axis_size("expert")
@@ -113,6 +118,353 @@
     return (velocity[None, None], rollout)
 
 
+def flipped(index, mask):
+    for bit in range(mask.bit_length()):
+        if (mask >> bit) & 1:
+            index = index + (1 - 2 * ((index // (1 << bit)) % 2)) * (1 << bit)
+    return index
+
+
+def fused_kernel(
+    depth, tok_hbm, grad_hbm, part_hbm, weight_hbm, momentum_hbm, velocity_hbm, rollout_hbm,
+    x_buf, g_buf, c_buf, w_buf, acc, vel, out_half, in_half, scaled, hidden_t, pre_grad_t,
+    ortho, gram, poly,
+    x_recv, g_recv, c_recv, row_send, local_sem, pair_send, pair_recv, sum_send, sum_recv,
+    roll_send, roll_recv, roll_local,
+):
+    rows, width = tok_hbm.shape
+    hidden_units = w_buf.shape[1]
+    me = lax.axis_index("expert")
+    pair = lax.axis_index("pair")
+    beside = {"expert": me + 1 - 2 * (me % 2)}
+    across = {"expert": flipped(me, 2)}
+    partner = {"pair": 1 - pair}
+    above = [{"expert": flipped(me // 4, d) * 4 + me % 4} for d in range(1, depth)]
+    mesh_id = pl.DeviceIdType.MESH
+
+    arrivals = ((x_buf, x_recv), (g_buf, g_recv), (c_buf, c_recv))
+    sent = []
+
+    def send(which, slot, to_slot, device):
+        buf, recv = arrivals[which]
+        copy = pltpu.make_async_remote_copy(
+            buf.at[slot], buf.at[to_slot], row_send.at[len(sent)], recv.at[to_slot],
+            device_id=device, device_id_type=mesh_id,
+        )
+        copy.start()
+        sent.append(copy)
+
+    def arrive(slot, which):
+        buf, recv = arrivals[which]
+        pltpu.make_async_remote_copy(
+            buf.at[slot], buf.at[slot], row_send.at[0], recv.at[slot],
+            device_id=beside, device_id_type=mesh_id,
+        ).wait_recv()
+
+    loads = [
+        pltpu.make_async_copy(source, target, local_sem.at[i])
+        for i, (source, target) in enumerate((
+            (tok_hbm, x_buf.at[0]), (grad_hbm, g_buf.at[0]), (part_hbm, c_buf.at[0]),
+            (weight_hbm.at[0, 0], w_buf.at[pair]), (momentum_hbm.at[0, 0], vel),
+        ))
+    ]
+    for load in loads:
+        load.start()
+    barrier = pltpu.get_barrier_semaphore()
+    near = above + [beside, across, partner]
+    for device in near:
+        pl.semaphore_signal(barrier, inc=1, device_id=device, device_id_type=mesh_id)
+    pl.semaphore_wait(barrier, len(near))
+    for load in loads[:3]:
+        load.wait()
+
+    for which in range(3):
+        send(which, 0, depth, beside)
+        send(which, 0, 2 * depth, across)
+        send(which, 0, 1, above[0])
+    for d in range(2, depth):
+        for which in range(3):
+            send(which, 0, d, above[d - 1])
+    loads[3].wait()
+    weight_copy = pltpu.make_async_remote_copy(
+        w_buf.at[pair], w_buf.at[pair], pair_send.at[0], pair_recv.at[0],
+        device_id=partner, device_id_type=mesh_id,
+    )
+    weight_copy.start()
+
+    tile = 256
+    n_hidden = hidden_units // tile
+    n_width = width // tile
+
+    def clear(i, carry):
+        part = pl.ds(pl.multiple_of(i * 128, 128), 128)
+        for m in range(2):
+            acc[m, part, :] = jnp.zeros((128, width), jnp.float32)
+        return carry
+
+    lax.fori_loop(0, hidden_units // 128, clear, 0)
+    for d in range(1, depth):
+        for which in range(3):
+            arrive(d, which)
+            send(which, d, depth + d, beside)
+            send(which, d, 2 * depth + d, across)
+    pltpu.make_async_remote_copy(
+        w_buf.at[pair], w_buf.at[1 - pair], pair_send.at[0], pair_recv.at[0],
+        device_id=partner, device_id_type=mesh_id,
+    ).wait_recv()
+
+    diagonal = lax.broadcasted_iota(jnp.int32, (rows, rows), 0) == lax.broadcasted_iota(
+        jnp.int32, (rows, rows), 1
+    )
+
+    def gradients(slot):
+        for i in range(2):
+            line = c_buf[slot + i, pl.ds(me, 1), :]
+            column = jnp.sum(jnp.where(diagonal, line, 0.0), axis=1, keepdims=True)
+
+            def scale(j, carry, i=i, column=column):
+                cols = pl.ds(pl.multiple_of(j * tile, tile), tile)
+                scaled[i * rows:(i + 1) * rows, cols] = (
+                    g_buf[slot + i, :, cols].astype(jnp.float32) * column
+                ).astype(jnp.bfloat16)
+                return carry
+
+            lax.fori_loop(0, n_width, scale, 0)
+
+        def activate(i, carry):
+            part = pl.ds(pl.multiple_of(i * tile, tile), tile)
+            x_rows = x_buf[pl.ds(slot, 2)].reshape(2 * rows, width)
+            pre = contract_last(x_rows, w_buf[0, part, :]) * (1.0 / math.sqrt(width))
+            hidden_grad = contract_last(scaled[...], w_buf[1, part, :]) * (
+                1.0 / math.sqrt(hidden_units)
+            )
+            squash = jax.nn.sigmoid(pre)
+            hidden_t[part, :] = (pre * squash).T.astype(jnp.bfloat16)
+            pre_grad_t[part, :] = (
+                hidden_grad * squash * (1.0 + pre * (1.0 - squash))
+            ).T.astype(jnp.bfloat16)
+            return carry
+
+        lax.fori_loop(0, n_hidden, activate, 0)
+
+        def outer(j, carry):
+            cols = pl.ds(pl.multiple_of(j * tile, tile), tile)
+            x_cols = x_buf[pl.ds(slot, 2), :, cols].reshape(2 * rows, tile)
+            acc[0, :, cols] += jnp.dot(
+                pre_grad_t[...], x_cols, preferred_element_type=jnp.float32
+            )
+            acc[1, :, cols] += jnp.dot(
+                hidden_t[...], scaled[:, cols], preferred_element_type=jnp.float32
+            )
+            return carry
+
+        lax.fori_loop(0, n_width, outer, 0)
+
+    def several(first, stride, count):
+        def one(i, carry):
+            gradients(first + i * stride)
+            return carry
+
+        lax.fori_loop(0, count, one, 0)
+
+    several(0, 2, depth // 2)
+    for d in range(0, depth, 2):
+        for k in (d, d + 1):
+            arrive(depth + k, 1)
+            send(1, depth + k, 3 * depth + k, across)
+            arrive(2 * depth + k, 0)
+            send(0, 2 * depth + k, 3 * depth + k, beside)
+            arrive(2 * depth + k, 2)
+            send(2, 2 * depth + k, 3 * depth + k, beside)
+        for k in (d, d + 1):
+            arrive(depth + k, 0)
+            arrive(depth + k, 2)
+            arrive(2 * depth + k, 1)
+        several(depth + d, depth, 2)
+    for d in range(0, depth, 2):
+        for k in (d, d + 1):
+            for which in range(3):
+                arrive(3 * depth + k, which)
+        gradients(3 * depth + d)
+
+    inv_width, inv_hidden = 1.0 / math.sqrt(width), 1.0 / math.sqrt(hidden_units)
+    own_scale = jnp.where(pair == 0, inv_width, inv_hidden).astype(jnp.float32)
+    other_scale = jnp.where(pair == 0, inv_hidden, inv_width).astype(jnp.float32)
+
+    def sum_copy(t):
+        part = pl.ds(pl.multiple_of(t * 128, 128), 128)
+        return pltpu.make_async_remote_copy(
+            out_half.at[part], in_half.at[part], sum_send.at[t], sum_recv.at[t],
+            device_id=partner, device_id_type=mesh_id,
+        )
+
+    def give(t, carry):
+        part = pl.ds(pl.multiple_of(t * 128, 128), 128)
+        out_half[part, :] = (acc[1 - pair, part, :] * other_scale).astype(jnp.bfloat16)
+        sum_copy(t).start()
+        return carry
+
+    steps = hidden_units // 128
+    lax.fori_loop(0, steps, give, 0)
+    loads[4].wait()
+
+    def take(t, squares):
+        part = pl.ds(pl.multiple_of(t * 128, 128), 128)
+        sum_copy(t).wait_recv()
+        new = DECAY * vel[part, :] + (
+            acc[pair, part, :] * own_scale + in_half[part, :].astype(jnp.float32)
+        )
+        vel[part, :] = new
+        return squares + jnp.sum(new * new, axis=0, keepdims=True)
+
+    squares = lax.fori_loop(0, steps, take, jnp.zeros((1, width), jnp.float32))
+    store = pltpu.make_async_copy(vel, velocity_hbm.at[0, 0], local_sem.at[5])
+    store.start()
+    inverse = 1.0 / (jnp.sqrt(jnp.sum(squares, axis=1, keepdims=True)) + NORM_EPS)
+
+    def normalise(t, carry):
+        part = pl.ds(pl.multiple_of(t * 128, 128), 128)
+        ortho[part, :] = (vel[part, :] * inverse).astype(jnp.bfloat16)
+        sum_copy(t).wait_send()
+        return carry
+
+    lax.fori_loop(0, steps, normalise, 0)
+
+    half = hidden_units // 2
+    step_size = 0.5 * math.sqrt(width)
+
+    def roll_copies(j):
+        cols = pl.ds(pl.multiple_of(j * tile, tile), tile)
+        away = pltpu.make_async_remote_copy(
+            out_half.at[pl.ds(pl.multiple_of((1 - pair) * half, 128), half), cols],
+            rollout_hbm.at[pair, 0, :, cols], roll_send.at[j], roll_recv.at[j],
+            device_id=partner, device_id_type=mesh_id,
+        )
+        back = pltpu.make_async_remote_copy(
+            out_half.at[pl.ds(pl.multiple_of((1 - pair) * half, 128), half), cols],
+            rollout_hbm.at[1 - pair, 0, :, cols], roll_send.at[j], roll_recv.at[j],
+            device_id=partner, device_id_type=mesh_id,
+        )
+        stay = pltpu.make_async_copy(
+            out_half.at[pl.ds(pl.multiple_of(pair * half, 128), half), cols],
+            rollout_hbm.at[pair, 0, :, cols], roll_local.at[j],
+        )
+        return away, back, stay
+
+    for iteration in range(NS_ITERS):
+        def gram_rows(i, carry):
+            part = pl.ds(pl.multiple_of(i * tile, tile), tile)
+            gram[part, :] = contract_last(ortho[part, :], ortho[...]).astype(jnp.bfloat16)
+            return carry
+
+        lax.fori_loop(0, n_hidden, gram_rows, 0)
+
+        def poly_rows(i, carry):
+            part = pl.ds(pl.multiple_of(i * tile, tile), tile)
+            square = jnp.dot(gram[part, :], gram[...], preferred_element_type=jnp.float32)
+            poly[part, :] = (COEF_B * gram[part, :].astype(jnp.float32) + COEF_C * square).astype(
+                jnp.bfloat16
+            )
+            return carry
+
+        lax.fori_loop(0, n_hidden, poly_rows, 0)
+
+        def advance(j, carry, last=iteration == NS_ITERS - 1):
+            cols = pl.ds(pl.multiple_of(j * tile, tile), tile)
+            old = ortho[:, cols]
+            new = (
+                COEF_A * old.astype(jnp.float32)
+                + jnp.dot(poly[...], old, preferred_element_type=jnp.float32)
+            ).astype(jnp.bfloat16)
+            if last:
+                out_half[:, cols] = (
+                    w_buf[pair, :, cols].astype(jnp.float32) - step_size * new.astype(jnp.float32)
+                ).astype(jnp.bfloat16)
+                away, _, stay = roll_copies(j)
+                away.start()
+                stay.start()
+            else:
+                ortho[:, cols] = new
+            return carry
+
+        lax.fori_loop(0, n_width, advance, 0)
+
+    for copy in sent:
+        copy.wait_send()
+    weight_copy.wait_send()
+
+    def finish(j, carry):
+        away, back, stay = roll_copies(j)
+        away.wait_send()
+        back.wait_recv()
+        stay.wait()
+        return carry
+
+    lax.fori_loop(0, n_width, finish, 0)
+    store.wait()
+
+
+def fused(tokens, out_grads, routing, combine, weights, momentum):
+    n_expert = lax.axis_size("expert")
+    depth = n_expert // 4
+    rows, width = tokens.shape
+    hidden_units = weights.shape[2]
+    slots = 4 * depth
+    names = jnp.arange(n_expert, dtype=jnp.int32)[:, None, None]
+    row_weight = jnp.sum(jnp.where(routing[None] == names, combine[None], 0.0), axis=2)
+    half_shape = (2, 1, hidden_units // 2, width)
+    any_space = pl.BlockSpec(memory_space=pl.ANY)
+    matrix = (hidden_units, width)
+    sends = 3 * (depth - 1) + 9 * depth
+    dma = pltpu.SemaphoreType.DMA
+    return pl.pallas_call(
+        functools.partial(fused_kernel, depth),
+        out_shape=(
+            jax.ShapeDtypeStruct(momentum.shape, jnp.float32),
+            jax.ShapeDtypeStruct(half_shape, jnp.bfloat16),
+        ),
+        in_specs=[any_space] * 5,
+        out_specs=(any_space, any_space),
+        scratch_shapes=[
+            pltpu.VMEM((slots, rows, width), jnp.bfloat16),
+            pltpu.VMEM((slots, rows, width), jnp.bfloat16),
+            pltpu.VMEM((slots, n_expert, rows), jnp.float32),
+            pltpu.VMEM((2,) + matrix, jnp.bfloat16),
+            pltpu.VMEM((2,) + matrix, jnp.float32),
+            pltpu.VMEM(matrix, jnp.float32),
+            pltpu.VMEM(matrix, jnp.bfloat16),
+            pltpu.VMEM(matrix, jnp.bfloat16),
+            pltpu.VMEM((2 * rows, width), jnp.bfloat16),
+            pltpu.VMEM((hidden_units, 2 * rows), jnp.bfloat16),
+            pltpu.VMEM((hidden_units, 2 * rows), jnp.bfloat16),
+            pltpu.VMEM(matrix, jnp.bfloat16),
+            pltpu.VMEM((hidden_units, hidden_units), jnp.bfloat16),
+            pltpu.VMEM((hidden_units, hidden_units), jnp.bfloat16),
+            dma((slots,)),
+            dma((slots,)),
+            dma((slots,)),
+            dma((sends,)),
+            dma((6,)),
+            dma((1,)),
+            dma((1,)),
+            dma((hidden_units // 128,)),
+            dma((hidden_units // 128,)),
+            dma((width // 256,)),
+            dma((width // 256,)),
+            dma((width // 256,)),
+        ],
+        compiler_params=pltpu.CompilerParams(
+            collective_id=0, has_side_effects=True, vmem_limit_bytes=VMEM_BYTES
+        ),
+    )(tokens, out_grads, row_weight, weights, momentum)
+
+
+def on_device(tokens, out_grads, routing, combine, weights, momentum):
+    gathered_bytes = 2 * tokens.size * tokens.dtype.itemsize * lax.axis_size("expert")
+    step = fused if gathered_bytes <= GATHER_LIMIT else exchanged
+    return step(tokens, out_grads, routing, combine, weights, momentum)
+
+
 def solution(mesh):
     return jax.shard_map(
         on_device,

time: 502 us -> 198 us (0.39); the launches traced: 494 us -> 198 us
  waiting for transfers between devices: 227 us -> 0 us
  Pallas kernels: 0 us -> 188 us
  local copies, waits for them, and re-layouts: 79.7 us -> 8.1 us
  matrix products: 71.3 us -> 0 us
  other arithmetic: 54.2 us -> 1.32 us
  starting transfers between devices: 36.3 us -> 0 us
  between operations: 15.4 us -> 0.65 us
  blocking collectives: 10.3 us -> 0 us
    all_to_all x2 -> x0, waiting for transfers between devices: 191 us -> none  [the longest x1 99.9 us: on_device(): lax.all_to_all(x_send, 'expert', split_axis=0, concat_axis=0, tiled=True)]
    pallas_call x0 -> x1, Pallas kernels: none -> 188 us  [fused(): pl.pallas_call(functools.partial(fused_kernel, depth), out_shape=(jax.Sha...]
    dot_general x7 -> x0, matrix products: 71.3 us -> none  [the longest x2 32.5 us: contract_first(): lax.dot_general(left_side, right_side, (((0,), (0,)), ((), ())), preferre...]
    all_to_all x2 -> x0, starting transfers between devices: 36.2 us -> none  [the longest x1 27.2 us: on_device(): lax.all_to_all(x_send, 'expert', split_axis=0, concat_axis=0, tiled=True)]
    reduce_scatter x1 -> x0, waiting for transfers between devices: 35.1 us -> none  [on_device(): lax.psum_scatter(jnp.stack([grad_up, grad_down])[:, None].astype(jnp.bflo...]
    unnamed x1 -> x0, other arithmetic: 20.5 us -> none
    gather x3 -> x0, local copies, waits for them, and re-layouts: 18.4 us -> none  [the longest x2 11.7 us: on_device(): tokens[slot_token]]
    scatter x3 -> x0, local copies, waits for them, and re-layouts: 13 us -> none  [the longest x1 4.34 us: on_device(): filled = jnp.zeros((slot_count,), jnp.bool_).at[target].set(True)]
  transfers between devices with their start and end apart: 4 -> 0, of which waited for: 3 -> 0; matrix products, arithmetic and copies ran while one was open for 6% -> 0% of each run, Pallas kernels for 0% -> 0%
where the time goes in v2:
time: 198 us
  Pallas kernels  188 us (95%)
  local copies, waits for them, and re-layouts  8.1 us (4%)
    pallas_call x1, Pallas kernels, fused(): pl.pallas_call(functools.partial(fused_kernel, depth), out_shape=(jax.Sha...  188 us
    unnamed x4, local copies, waits for them, and re-layouts  8.1 us

profile of v2, /device:TPU:0, one launch (start us, length us, event | category | flops | bytes accessed | tf_op | source)
XLA Modules:
  0.0 198.1 jit_solution(10315349029505541199)
XLA Ops:
  0.6 1.3 select_reduce_fusion.part_hbm
  2.0 188.0 %shard_map.77 = (f32[1,1,768,2048]{3,2,1,0:T(8,128)}, bf16[2,1,384,2048]{3,2,1,0:T(8,128)(2,1)}) custom-call(bf16[128,2048]{1,0:T(8,128)(2,1)} %tok_hbm.1, bf16[128,2048]{1,0:T(8,128)(2,1)} %grad_hbm.1, f32[16,128]{1,0:T(8,128)} %select_reduce_fusion.part_hbm, bf16[1,1,768,2048]{3,2,1,0:T(8,128)(2,1)} %weight_hbm.1, f32[1,1,768,2048]{3,2,1,0:T(8,128)} %momentum_hbm.1), custom_call_target="tpu_custom_call" | custom-call | tf_op jit(solution)/shard_map/pallas_call | solution.py:420
  190.0 0.0 copy-start
  190.0 6.4 %copy.12 = f32[1,1,768,2048]{3,2,1,0:T(8,128)} copy(f32[1,1,768,2048]{3,2,1,0:T(8,128)} %get-tuple-element.4) | data formatting | bytes 12582912
  196.5 0.0 copy-done
  196.5 1.7 copy.13
Async XLA Ops:
  190.0 6.4 %copy-start = (bf16[2,1,384,2048]{3,2,1,0:T(8,128)(2,1)S(1)}, bf16[2,1,384,2048]{3,2,1,0:T(8,128)(2,1)}, u32[]{:S(2)}) copy-start(bf16[2,1,384,2048]{3,2,1,0:T(8,128)(2,1)} %get-tuple-element.5) | copy-start | bytes 9437188

commit v3 on v2

--- a/solution.py
+++ b/solution.py
@@ -127,7 +127,7 @@
 
 def fused_kernel(
     depth, tok_hbm, grad_hbm, part_hbm, weight_hbm, momentum_hbm, velocity_hbm, rollout_hbm,
-    x_buf, g_buf, c_buf, w_buf, acc, vel, out_half, in_half, scaled, hidden_t, pre_grad_t,
+    x_buf, g_buf, c_buf, w_buf, acc, vel, out_half, in_half, row_pair, slope,
     ortho, gram, poly,
     x_recv, g_recv, c_recv, row_send, local_sem, pair_send, pair_recv, sum_send, sum_recv,
     roll_send, roll_recv, roll_local,
@@ -145,19 +145,23 @@
     arrivals = ((x_buf, x_recv), (g_buf, g_recv), (c_buf, c_recv))
     sent = []
 
-    def send(which, slot, to_slot, device):
-        buf, recv = arrivals[which]
+    def piece(which, slot, upper):
+        ref = arrivals[which][0].at[slot]
+        return ref if upper is None else ref.at[pl.ds(upper * (rows // 2), rows // 2)]
+
+    def send(which, slot, to_slot, device, upper=None):
         copy = pltpu.make_async_remote_copy(
-            buf.at[slot], buf.at[to_slot], row_send.at[len(sent)], recv.at[to_slot],
+            piece(which, slot, upper), piece(which, to_slot, upper), row_send.at[len(sent)],
+            arrivals[which][1].at[to_slot + (upper or 0)],
             device_id=device, device_id_type=mesh_id,
         )
         copy.start()
         sent.append(copy)
 
-    def arrive(slot, which):
-        buf, recv = arrivals[which]
+    def arrive(slot, which, upper=None):
+        part = piece(which, slot, upper)
         pltpu.make_async_remote_copy(
-            buf.at[slot], buf.at[slot], row_send.at[0], recv.at[slot],
+            part, part, row_send.at[0], arrivals[which][1].at[slot + (upper or 0)],
             device_id=beside, device_id_type=mesh_id,
         ).wait_recv()
 
@@ -202,12 +206,28 @@
             acc[m, part, :] = jnp.zeros((128, width), jnp.float32)
         return carry
 
-    lax.fori_loop(0, hidden_units // 128, clear, 0)
-    for d in range(1, depth):
+    def relay(k, upper=None):
+        arrive(depth + k, 1)
+        send(1, depth + k, 3 * depth + k, across, upper)
+        arrive(2 * depth + k, 0)
+        send(0, 2 * depth + k, 3 * depth + k, beside, upper)
+        arrive(2 * depth + k, 2)
+        send(2, 2 * depth + k, 3 * depth + k, beside)
+
+    def rest(k):
+        arrive(depth + k, 0)
+        arrive(depth + k, 2)
+        arrive(2 * depth + k, 1)
+
+    def column(d):
         for which in range(3):
             arrive(d, which)
             send(which, d, depth + d, beside)
             send(which, d, 2 * depth + d, across)
+
+    lax.fori_loop(0, hidden_units // 128, clear, 0)
+    relay(0)
+    column(1)
     pltpu.make_async_remote_copy(
         w_buf.at[pair], w_buf.at[1 - pair], pair_send.at[0], pair_recv.at[0],
         device_id=partner, device_id_type=mesh_id,
@@ -217,14 +237,14 @@
         jnp.int32, (rows, rows), 1
     )
 
-    def gradients(slot):
+    def activations(slot):
         for i in range(2):
             line = c_buf[slot + i, pl.ds(me, 1), :]
             column = jnp.sum(jnp.where(diagonal, line, 0.0), axis=1, keepdims=True)
 
             def scale(j, carry, i=i, column=column):
                 cols = pl.ds(pl.multiple_of(j * tile, tile), tile)
-                scaled[i * rows:(i + 1) * rows, cols] = (
+                row_pair[1, i * rows:(i + 1) * rows, cols] = (
                     g_buf[slot + i, :, cols].astype(jnp.float32) * column
                 ).astype(jnp.bfloat16)
                 return carry
@@ -235,26 +255,29 @@
             part = pl.ds(pl.multiple_of(i * tile, tile), tile)
             x_rows = x_buf[pl.ds(slot, 2)].reshape(2 * rows, width)
             pre = contract_last(x_rows, w_buf[0, part, :]) * (1.0 / math.sqrt(width))
-            hidden_grad = contract_last(scaled[...], w_buf[1, part, :]) * (
+            hidden_grad = contract_last(row_pair[1], w_buf[1, part, :]) * (
                 1.0 / math.sqrt(hidden_units)
             )
             squash = jax.nn.sigmoid(pre)
-            hidden_t[part, :] = (pre * squash).T.astype(jnp.bfloat16)
-            pre_grad_t[part, :] = (
+            slope[1, part, :] = (pre * squash).T.astype(jnp.bfloat16)
+            slope[0, part, :] = (
                 hidden_grad * squash * (1.0 + pre * (1.0 - squash))
             ).T.astype(jnp.bfloat16)
             return carry
 
         lax.fori_loop(0, n_hidden, activate, 0)
+
+    def gradients(slot):
+        activations(slot)
 
         def outer(j, carry):
             cols = pl.ds(pl.multiple_of(j * tile, tile), tile)
             x_cols = x_buf[pl.ds(slot, 2), :, cols].reshape(2 * rows, tile)
             acc[0, :, cols] += jnp.dot(
-                pre_grad_t[...], x_cols, preferred_element_type=jnp.float32
+                slope[0], x_cols, preferred_element_type=jnp.float32
             )
             acc[1, :, cols] += jnp.dot(
-                hidden_t[...], scaled[:, cols], preferred_element_type=jnp.float32
+                slope[1], row_pair[1, :, cols], preferred_element_type=jnp.float32
             )
             return carry
 
@@ -267,57 +290,76 @@
 
         lax.fori_loop(0, count, one, 0)
 
-    several(0, 2, depth // 2)
-    for d in range(0, depth, 2):
-        for k in (d, d + 1):
-            arrive(depth + k, 1)
-            send(1, depth + k, 3 * depth + k, across)
-            arrive(2 * depth + k, 0)
-            send(0, 2 * depth + k, 3 * depth + k, beside)
-            arrive(2 * depth + k, 2)
-            send(2, 2 * depth + k, 3 * depth + k, beside)
-        for k in (d, d + 1):
-            arrive(depth + k, 0)
-            arrive(depth + k, 2)
-            arrive(2 * depth + k, 1)
+    last = depth - 1
+    gradients(0)
+    for d in range(2, depth, 2):
+        column(d)
+        if d == 2:
+            for which in range(3):
+                arrive(3 * depth, which)
+                send(which, 3 * depth, 3 * depth + 1, above[0])
+            for which in range(2):
+                send(which, 3 * depth, 3 * depth + last, above[last - 1], 0)
+            for which in range(3):
+                arrive(depth + 1, which)
+                arrive(2 * depth + 1, which)
+            rest(0)
+            several(depth, depth, 2)
+        column(d + 1)
+        gradients(d)
+        relay(d)
+        relay(d + 1, 1 if d + 1 == last else None)
+        rest(d)
+        rest(d + 1)
         several(depth + d, depth, 2)
     for d in range(0, depth, 2):
         for k in (d, d + 1):
             for which in range(3):
-                arrive(3 * depth + k, which)
-        gradients(3 * depth + d)
+                if which < 2 and k == last:
+                    arrive(3 * depth + k, which, 0)
+                    arrive(3 * depth + k, which, 1)
+                elif k > 0:
+                    arrive(3 * depth + k, which)
+        if d + 2 < depth:
+            gradients(3 * depth + d)
+    final = 4 * depth - 2
+    activations(final)
+    row_pair[0] = x_buf[final:final + 2].reshape(2 * rows, width)
 
     inv_width, inv_hidden = 1.0 / math.sqrt(width), 1.0 / math.sqrt(hidden_units)
     own_scale = jnp.where(pair == 0, inv_width, inv_hidden).astype(jnp.float32)
     other_scale = jnp.where(pair == 0, inv_hidden, inv_width).astype(jnp.float32)
 
-    def sum_copy(t):
-        part = pl.ds(pl.multiple_of(t * 128, 128), 128)
+    def sum_copy(j):
+        cols = pl.ds(pl.multiple_of(j * tile, tile), tile)
         return pltpu.make_async_remote_copy(
-            out_half.at[part], in_half.at[part], sum_send.at[t], sum_recv.at[t],
+            out_half.at[:, cols], in_half.at[:, cols], sum_send.at[j], sum_recv.at[j],
             device_id=partner, device_id_type=mesh_id,
         )
 
-    def give(t, carry):
-        part = pl.ds(pl.multiple_of(t * 128, 128), 128)
-        out_half[part, :] = (acc[1 - pair, part, :] * other_scale).astype(jnp.bfloat16)
-        sum_copy(t).start()
+    def total(m, cols):
+        return acc[m, :, cols] + jnp.dot(
+            slope[m], row_pair[m, :, cols], preferred_element_type=jnp.float32
+        )
+
+    def give(j, carry):
+        cols = pl.ds(pl.multiple_of(j * tile, tile), tile)
+        out_half[:, cols] = (total(1 - pair, cols) * other_scale).astype(jnp.bfloat16)
+        sum_copy(j).start()
         return carry
 
-    steps = hidden_units // 128
-    lax.fori_loop(0, steps, give, 0)
+    lax.fori_loop(0, n_width, give, 0)
     loads[4].wait()
 
-    def take(t, squares):
-        part = pl.ds(pl.multiple_of(t * 128, 128), 128)
-        sum_copy(t).wait_recv()
-        new = DECAY * vel[part, :] + (
-            acc[pair, part, :] * own_scale + in_half[part, :].astype(jnp.float32)
-        )
-        vel[part, :] = new
+    def take(j, squares):
+        cols = pl.ds(pl.multiple_of(j * tile, tile), tile)
+        own = DECAY * vel[:, cols] + total(pair, cols) * own_scale
+        sum_copy(j).wait_recv()
+        new = own + in_half[:, cols].astype(jnp.float32)
+        vel[:, cols] = new
         return squares + jnp.sum(new * new, axis=0, keepdims=True)
 
-    squares = lax.fori_loop(0, steps, take, jnp.zeros((1, width), jnp.float32))
+    squares = lax.fori_loop(0, n_width, take, jnp.zeros((1, tile), jnp.float32))
     store = pltpu.make_async_copy(vel, velocity_hbm.at[0, 0], local_sem.at[5])
     store.start()
     inverse = 1.0 / (jnp.sqrt(jnp.sum(squares, axis=1, keepdims=True)) + NORM_EPS)
@@ -325,10 +367,15 @@
     def normalise(t, carry):
         part = pl.ds(pl.multiple_of(t * 128, 128), 128)
         ortho[part, :] = (vel[part, :] * inverse).astype(jnp.bfloat16)
-        sum_copy(t).wait_send()
         return carry
 
-    lax.fori_loop(0, steps, normalise, 0)
+    lax.fori_loop(0, hidden_units // 128, normalise, 0)
+
+    def sum_sent(j, carry):
+        sum_copy(j).wait_send()
+        return carry
+
+    lax.fori_loop(0, n_width, sum_sent, 0)
 
     half = hidden_units // 2
     step_size = 0.5 * math.sqrt(width)
@@ -415,7 +462,7 @@
     half_shape = (2, 1, hidden_units // 2, width)
     any_space = pl.BlockSpec(memory_space=pl.ANY)
     matrix = (hidden_units, width)
-    sends = 3 * (depth - 1) + 9 * depth
+    sends = 3 * (depth - 1) + 9 * depth + 2
     dma = pltpu.SemaphoreType.DMA
     return pl.pallas_call(
         functools.partial(fused_kernel, depth),
@@ -434,21 +481,20 @@
             pltpu.VMEM(matrix, jnp.float32),
             pltpu.VMEM(matrix, jnp.bfloat16),
             pltpu.VMEM(matrix, jnp.bfloat16),
-            pltpu.VMEM((2 * rows, width), jnp.bfloat16),
-            pltpu.VMEM((hidden_units, 2 * rows), jnp.bfloat16),
-            pltpu.VMEM((hidden_units, 2 * rows), jnp.bfloat16),
+            pltpu.VMEM((2, 2 * rows, width), jnp.bfloat16),
+            pltpu.VMEM((2, hidden_units, 2 * rows), jnp.bfloat16),
             pltpu.VMEM(matrix, jnp.bfloat16),
             pltpu.VMEM((hidden_units, hidden_units), jnp.bfloat16),
             pltpu.VMEM((hidden_units, hidden_units), jnp.bfloat16),
-            dma((slots,)),
-            dma((slots,)),
+            dma((slots + 1,)),
+            dma((slots + 1,)),
             dma((slots,)),
             dma((sends,)),
             dma((6,)),
             dma((1,)),
             dma((1,)),
-            dma((hidden_units // 128,)),
-            dma((hidden_units // 128,)),
+            dma((width // 256,)),
+            dma((width // 256,)),
             dma((width // 256,)),
             dma((width // 256,)),
             dma((width // 256,)),

time: 198 us -> 171 us (0.86)
  Pallas kernels: 188 us -> 160 us
    pallas_call x1, Pallas kernels: 188 us -> 160 us  [fused(): pl.pallas_call(functools.partial(fused_kernel, depth), out_shape=(jax.Sha...]
where the time goes in v3:
time: 171 us; the launch traced here: 170 us
  Pallas kernels  160 us (94%)
  local copies, waits for them, and re-layouts  8.1 us (5%)
    pallas_call x1, Pallas kernels, fused(): pl.pallas_call(functools.partial(fused_kernel, depth), out_shape=(jax.Sha...  160 us
    unnamed x4, local copies, waits for them, and re-layouts  8.1 us

profile of v3, /device:TPU:0, one launch (start us, length us, event | category | flops | bytes accessed | tf_op | source)
XLA Modules:
  0.0 170.3 jit_solution(11122979639634001779)
XLA Ops:
  0.6 1.3 select_reduce_fusion.part_hbm
  2.0 160.2 %shard_map.77 = (f32[1,1,768,2048]{3,2,1,0:T(8,128)}, bf16[2,1,384,2048]{3,2,1,0:T(8,128)(2,1)}) custom-call(bf16[128,2048]{1,0:T(8,128)(2,1)} %tok_hbm.1, bf16[128,2048]{1,0:T(8,128)(2,1)} %grad_hbm.1, f32[16,128]{1,0:T(8,128)} %select_reduce_fusion.part_hbm, bf16[1,1,768,2048]{3,2,1,0:T(8,128)(2,1)} %weight_hbm.1, f32[1,1,768,2048]{3,2,1,0:T(8,128)} %momentum_hbm.1), custom_call_target="tpu_custom_call" | custom-call | tf_op jit(solution)/shard_map/pallas_call | solution.py:467
  162.2 0.0 copy-start
  162.2 6.4 %copy.12 = f32[1,1,768,2048]{3,2,1,0:T(8,128)} copy(f32[1,1,768,2048]{3,2,1,0:T(8,128)} %get-tuple-element.4) | data formatting | bytes 12582912
  168.6 0.0 copy-done
  168.6 1.7 copy.13
Async XLA Ops:
  162.2 6.4 %copy-start = (bf16[2,1,384,2048]{3,2,1,0:T(8,128)(2,1)S(1)}, bf16[2,1,384,2048]{3,2,1,0:T(8,128)(2,1)}, u32[]{:S(2)}) copy-start(bf16[2,1,384,2048]{3,2,1,0:T(8,128)(2,1)} %get-tuple-element.5) | copy-start | bytes 9437188
